TPU v7x, 32 devices: a whole 2x2x4 slice. The times are simulated.
32 devices in a mesh: groups: 2 (over y), ctx: 16 (over z, x, core).
Axes of the slice: x: 2, y: 2, z: 4, core: 2. Of those that a mesh axis runs over, the one named last changes fastest.
Arguments:
- q_nope: bfloat16 [4096, 8192], P(('groups', 'ctx')), parts along dimension 0, may hold values from -6 to 6
- q_rope: bfloat16 [4096, 4096], P(('groups', 'ctx')), parts along dimension 0, may hold values from -240 to 240
- latent: bfloat16 [4096, 576], P(('groups', 'ctx')), parts along dimension 0, may hold values from -4 to 4
- w_uk: bfloat16 [512, 8192], P('ctx'), may hold values from -0.5 to 0.5
- w_uv: bfloat16 [512, 8192], P('ctx'), may hold values from -0.25 to 0.25
- doc_lengths: int32 [16], P('groups'), parts along dimension 0, may hold values from 1 to 512, 2048 in all
Outputs:
- attended: bfloat16 [4096, 8192], P(('groups', 'ctx')), parts along dimension 0
There are 2 independent parts, one for each index of `groups`. A program takes and returns all parts, laid end to end along the dimension named above; an argument that names none is the same for every part. Nothing has to cross between parts.
Inputs may be any that keep to these rules, and one draw needn't show every extreme that they name: `doc_lengths`: the documents fill the context exactly, and one of them has 512 tokens.
All inputs are finite; a program needn't handle non-finite values.
Results may differ from a plain program's by a relative error of at most 0.0065.
Values may be sent and summed in bfloat16 or wider, within the bound.
A program may use at most 128 MiB of HBM per device.

v0:
```python
import math

import jax
import jax.numpy as jnp
from jax import lax
from jax.sharding import PartitionSpec as P

HEADS = 64
DN = 128
DV = 128
DR = 64
LAT = 512
SPAN = 4


def from_behind(block, axis, distance):
    devices = range(lax.axis_size(axis))
    route = [(i - distance, i) for i in devices if i - distance in devices]
    return lax.ppermute(block, axis, route)


def doc_index(starts, positions):
    return jnp.sum((starts[None, :] <= positions[:, None]).astype(jnp.int32), axis=1) - 1


def allowed_pairs(starts, key_start, key_count, q_pos, q_doc):
    k_pos = key_start + jnp.arange(key_count, dtype=jnp.int32)
    k_doc = doc_index(starts, k_pos)
    return (q_doc[:, None] == k_doc[None, :]) & (k_pos[None, :] <= q_pos[:, None])


def attend(state, keys, allowed, absorbed, rope_q, scale):
    top, total, summed = state
    scores = jnp.einsum("thj,kj->thk", absorbed, keys[:, :LAT], preferred_element_type=jnp.float32)
    scores = scores + jnp.einsum(
        "thr,kr->thk", rope_q, keys[:, LAT:], preferred_element_type=jnp.float32
    )
    scores = scores * scale
    mask = allowed[:, None, :]
    fresh = jnp.maximum(top, jnp.max(jnp.where(mask, scores, jnp.float32(-1e30)), axis=-1))
    weights = jnp.where(mask, jnp.exp(scores - fresh[..., None]), jnp.float32(0.0))
    factor = jnp.exp(top - fresh)
    total = total * factor + jnp.sum(weights, axis=-1)
    summed = summed * factor[..., None] + jnp.einsum(
        "thk,kj->thj",
        weights.astype(jnp.bfloat16),
        keys[:, :LAT],
        preferred_element_type=jnp.float32,
    )
    return (fresh, total, summed)


def shards(q_nope, q_rope, latent, w_uk, w_uv, doc_lengths):
    rows_here = q_nope.shape[0]
    scale = 1.0 / math.sqrt(DN + DR)
    place = lax.axis_index("ctx")
    queries = q_nope.reshape(rows_here, HEADS, DN)
    rope_q = q_rope.reshape(rows_here, HEADS, DR)
    piece = lax.all_gather(w_uk, "ctx", axis=0, tiled=True)
    weights = piece.reshape(piece.shape[0], HEADS, DN)
    absorbed = jnp.einsum(
        "thd,jhd->thj", queries, weights, preferred_element_type=jnp.float32
    ).astype(jnp.bfloat16)
    starts = jnp.cumsum(doc_lengths) - doc_lengths
    q_pos = place * rows_here + jnp.arange(rows_here, dtype=jnp.int32)
    q_doc = doc_index(starts, q_pos)
    state = (
        jnp.full((rows_here, HEADS), -1e30, jnp.float32),
        jnp.zeros((rows_here, HEADS), jnp.float32),
        jnp.zeros((rows_here, HEADS, LAT), jnp.float32),
    )

    def take_block(carry, keys, key_start):
        allowed = allowed_pairs(starts, key_start, keys.shape[0], q_pos, q_doc)
        return lax.cond(
            jnp.any(allowed),
            lambda value: attend(value, keys, allowed, absorbed, rope_q, scale),
            lambda value: value,
            carry,
        )

    state = take_block(state, latent, place * rows_here)
    moving = latent
    for back in range(1, SPAN + 1):
        moving = from_behind(moving, "ctx", 1)
        state = take_block(state, moving, (place - back) * rows_here)
    top, total, summed = state
    mixed = (summed / total[..., None]).astype(jnp.bfloat16)
    piece = lax.all_gather(w_uv, "ctx", axis=0, tiled=True)
    rows = piece.shape[0]
    weights = piece.reshape(rows, HEADS, DV)
    term = jnp.einsum("thj,jhd->thd", mixed, weights, preferred_element_type=jnp.float32)
    result = term.reshape(rows_here, HEADS * DV)
    return result.astype(jnp.bfloat16)


def solution(mesh):
    placed = (
        P(("groups", "ctx"), None),
        P(("groups", "ctx"), None),
        P(("groups", "ctx"), None),
        P("ctx", None),
        P("ctx", None),
        P("groups"),
    )
    return jax.shard_map(
        shards, mesh=mesh, in_specs=placed, out_specs=P(("groups", "ctx"), None), check_vma=False
    )
```

profile of v0, /device:TPU:8, one launch (start us, length us, event | category | flops | bytes accessed | tf_op | source)
XLA Modules:
  0.0 240.7 jit_solution(1552924104266842702)
XLA Ops:
  6.5 0.7 all-gather.3.cloned.1.call-update
  7.3 0.7 all-gather.5.cloned.1.call-update
  8.0 1.1 copy.90
  9.1 1.9 collective-permute-start
  11.0 1.6 copy.87
  12.6 0.8 reduce-window.9
  13.5 0.7 bitcast_subtract_fusion
  14.2 0.1 convert_reduce_fusion
  14.3 2.3 collective-permute-done
  16.6 1.9 collective-permute-start.1
  18.5 8.7 %collective-permute-done.1 = bf16[128,576]{1,0:T(8,128)(2,1)S(1)} collective-permute-done((bf16[128,576]{1,0:T(8,128)(2,1)S(1)}, bf16[128,576]{1,0:T(8,128)(2,1)S(1)}, u32[]{:S(2)}, u32[]{:S(2)}) %collective-permute-start.1) | collective-permute-done | bytes 147488 | tf_op jit(solution)/shard_map/ppermute | solution.py:19
  27.2 1.9 collective-permute-start.2
  29.2 1.5 compare_and_fusion
  33.7 4.7 %collective-permute-done.2 = bf16[128,576]{1,0:T(8,128)(2,1)} collective-permute-done((bf16[128,576]{1,0:T(8,128)(2,1)S(1)}, bf16[128,576]{1,0:T(8,128)(2,1)}, u32[]{:S(2)}, u32[]{:S(2)}) %collective-permute-start.2) | collective-permute-done | bytes 147488 | tf_op jit(solution)/shard_map/ppermute | solution.py:19
  38.4 1.9 collective-permute-start.3
  40.3 48.3 %all-gather.3.cloned.1.call-done = bf16[512,8192]{1,0:T(8,128)(2,1)} async-done(((bf16[32,8192]{1,0:T(8,128)(2,1)}), bf16[512,8192]{1,0:T(8,128)(2,1)}) %all-gather.3.cloned.1.call-update) | async-done | bytes 8388624 | tf_op jit(solution)/shard_map/all_gather | solution.py:59
  88.5 11.9 %copy.84 = bf16[512,8192]{0,1:T(8,128)(2,1)} copy(bf16[512,8192]{1,0:T(8,128)(2,1)} %all-gather.3.cloned.1.call-done) | data formatting | bytes 16777216 | tf_op jit(solution)/shard_map/all_gather | solution.py:59
  100.5 6.8 %convert_bitcast_fusion = bf16[128,64,512]{0,2,1:T(8,128)(2,1)} fusion(bf16[512,64,128]{0,2,1:T(8,128)(2,1)} %bitcast.84, bf16[128,8192]{1,0:T(8,128)(2,1)S(1)} %copy-done), kind=kOutput, calls=%fused_computation.90 | convolution fusion | flops 1077936128 | bytes 18874368 | tf_op jit(solution)/shard_map/thd,jhd->thj/dot_general | solution.py:61
  107.3 19.2 %conditional.5 = (f32[128,64]{0,1:T(8,128)}, f32[128,64]{0,1:T(8,128)S(1)}, f32[128,64,512]{2,0,1:T(8,128)}) conditional(s32[]{:T(128)} %convert_element_type.73, () %tuple.38, (pred[128,128]{0,1:T(8,128)(4,1)}, bf16[128,576]{0,1:T(8,128)(2,1)}, bf16[128,64,512]{0,2,1:T(8,128)(2,1)}, bf16[128,64,64]{0,2,1:T(8,128)(2,1)S(1)}) %tuple.116), branch_computations={%region_11.12_spmd, %region_12.0_spmd} | conditional | flops 2296414208 | bytes 48234548 | solution.py:75
  107.3 1.1 copy.88
  108.4 1.5 fusion.6
  109.9 5.5 %select_reduce_fusion = (f32[128,64]{0,1:T(8,128)S(1)}, f32[128,64,128]{0,2,1:T(8,128)S(1)}) fusion(pred[128,128]{0,1:T(8,128)(4,1)S(1)} %copy-done.5, f32[128,64,128]{0,2,1:T(8,128)S(1)} %fusion.6, bf16[128,64,512]{0,2,1:T(8,128)(2,1)} %get-tuple-element.249, bf16[128,576]{1,0:T(8,128)(2,1)S(1)} %copy.88), kind=kOutput, calls=%fused_computation.2 | convolution fusion | flops 1077927936 | bytes 16957440 | tf_op jit(solution)/shard_map/cond/branch_1_fun/thj,kj->thk/dot_general | solution.py:34
  115.4 0.6 exponential_multiply_fusion
  116.0 8.0 %convolution_add_fusion = f32[128,64,512]{2,0,1:T(8,128)} fusion(f32[128,64]{0,1:T(8,128)S(1)} %get-tuple-element.284, f32[128,64,128]{0,2,1:T(8,128)S(1)} %get-tuple-element.303, f32[128,64]{0,1:T(8,128)} %get-tuple-element.329, pred[128,128]{0,1:T(8,128)(4,1)S(1)} %copy-done.5, bf16[128,576]{1,0:T(8,128)(2,1)S(1)} %copy.88), kind=kOutput, calls=%fused_computation | convolution fusion | flops 1081081856 | bytes 21184512 | tf_op jit(solution)/shard_map/cond/branch_1_fun/thk,kj->thj/dot_general | solution.py:44
  124.0 1.7 fusion.1
  125.7 0.8 fusion.10
  126.5 20.2 %conditional.6 = ((f32[128,64]{0,1:T(8,128)}, f32[128,64]{0,1:T(8,128)S(1)}, f32[128,64,512]{2,0,1:T(8,128)})) conditional(s32[]{:T(128)} %convert_element_type.72, (f32[128,64]{0,1:T(8,128)}, f32[128,64]{0,1:T(8,128)S(1)}, f32[128,64,512]{2,0,1:T(8,128)}) %conditional.5, (pred[128,128]{0,1:T(8,128)(4,1)S(1)}, bf16[128,576]{1,0:T(8,128)(2,1)S(1)}, ...), branch_computations={%region_15.16_spmd, %region_16.19_spmd} | conditional | flops 2300592128 | bytes 65110048 | solution.py:75
  126.7 0.1 copy.76
  126.9 0.8 fusion.21
  127.6 5.3 %select_reduce_fusion.1 = (f32[128,64]{0,1:T(8,128)S(1)}, f32[128,64,128]{0,2,1:T(8,128)S(1)}) fusion(pred[128,128]{0,1:T(8,128)(4,1)S(1)} %get-tuple-element.96, f32[128,64,128]{0,2,1:T(8,128)S(1)} %fusion.21, bf16[128,64,512]{0,2,1:T(8,128)(2,1)} %get-tuple-element.253, bf16[128,576]{1,0:T(8,128)(2,1)S(1)} %get-tuple-element.98), kind=kOutput, calls=%fused_computation.19 | convolution fusion | flops 1077927936 | bytes 16957440 | tf_op jit(solution)/shard_map/cond/branch_1_fun/thj,kj->thk/dot_general | solution.py:34
  132.9 0.8 max.8
  133.7 0.9 fusion.12
  134.6 0.8 multiply_add_fusion.1
  135.4 10.7 %multiply_add_fusion = f32[128,64,512]{2,0,1:T(8,128)} fusion(f32[128,64,512]{2,0,1:T(8,128)} %get-tuple-element.101, f32[128,64]{0,1:T(8,128)S(1)} %get-tuple-element.287, f32[128,64,128]{0,2,1:T(8,128)S(1)} %get-tuple-element.305, f32[128,64]{0,1:T(8,128)S(1)} %max.8, pred[128,128]{0,1:T(8,128)(4,1)S(1)} %get-tuple-element.96, ...), kind=kOutput, calls=%fused_computation.17 | convolution fusion | flops 1085276160 | bytes 37961728 | tf_op jit(solution)/shard_map/cond/branch_1_fun/thk,kj->thj/dot_general | solution.py:44
  146.1 0.6 copy.122
  146.7 20.3 %conditional.7 = ((f32[128,64]{0,1:T(8,128)}, f32[128,64]{0,1:T(8,128)S(1)}, f32[128,64,512]{2,0,1:T(8,128)})) conditional(s32[]{:T(128)} %convert_element_type.70, (f32[128,64]{0,1:T(8,128)}, f32[128,64]{0,1:T(8,128)S(1)}, f32[128,64,512]{2,0,1:T(8,128)}) %get-tuple-element.354, (pred[128,128]{0,1:T(8,128)(4,1)S(1)}, ...), branch_computations={%region_19.20_spmd, %region_20.23_spmd} | conditional | flops 2300592128 | bytes 65110048 | solution.py:75
  146.7 0.1 copy.78
  146.8 0.8 fusion.33
  147.6 5.5 %select_reduce_fusion.2 = (f32[128,64]{0,1:T(8,128)S(1)}, f32[128,64,128]{0,2,1:T(8,128)S(1)}) fusion(pred[128,128]{0,1:T(8,128)(4,1)S(1)} %get-tuple-element.103, f32[128,64,128]{0,2,1:T(8,128)S(1)} %fusion.33, bf16[128,64,512]{0,2,1:T(8,128)(2,1)} %get-tuple-element.260, bf16[128,576]{1,0:T(8,128)(2,1)S(1)} %get-tuple-element.105), kind=kOutput, calls=%fused_computation.37 | convolution fusion | flops 1077927936 | bytes 16957440 | tf_op jit(solution)/shard_map/cond/branch_1_fun/thj,kj->thk/dot_general | solution.py:34
  153.1 0.8 max.9
  153.9 0.9 fusion.24
  154.8 0.8 multiply_add_fusion.3
  155.6 10.8 %multiply_add_fusion.2 = f32[128,64,512]{2,0,1:T(8,128)} fusion(f32[128,64,512]{2,0,1:T(8,128)} %get-tuple-element.108, f32[128,64]{0,1:T(8,128)S(1)} %get-tuple-element.289, f32[128,64,128]{0,2,1:T(8,128)S(1)} %get-tuple-element.307, f32[128,64]{0,1:T(8,128)S(1)} %max.9, pred[128,128]{0,1:T(8,128)(4,1)S(1)} %get-tuple-element.103, ...), kind=kOutput, calls=%fused_computation.35 | convolution fusion | flops 1085276160 | bytes 37961728 | tf_op jit(solution)/shard_map/cond/branch_1_fun/thk,kj->thj/dot_general | solution.py:44
  166.4 0.6 copy.128
  167.0 20.7 %conditional.8 = ((f32[128,64]{0,1:T(8,128)}, f32[128,64]{0,1:T(8,128)S(1)}, f32[128,64,512]{2,0,1:T(8,128)})) conditional(s32[]{:T(128)} %convert_element_type.68, (f32[128,64]{0,1:T(8,128)}, f32[128,64]{0,1:T(8,128)S(1)}, f32[128,64,512]{2,0,1:T(8,128)}) %get-tuple-element.355, (pred[128,128]{0,1:T(8,128)(4,1)S(1)}, bf16[128,576]{1,0:T(8,128)(2,1)}, ...), branch_computations={%region_23.24_spmd, %region_24.0_spmd} | conditional | flops 2300592128 | bytes 65110048 | solution.py:75
  167.0 1.1 copy.80
  168.1 0.8 fusion.45
  168.8 5.2 %select_reduce_fusion.3 = (f32[128,64]{0,1:T(8,128)S(1)}, f32[128,64,128]{0,2,1:T(8,128)S(1)}) fusion(pred[128,128]{0,1:T(8,128)(4,1)S(1)} %get-tuple-element.110, f32[128,64,128]{0,2,1:T(8,128)S(1)} %fusion.45, bf16[128,64,512]{0,2,1:T(8,128)(2,1)} %get-tuple-element.267, bf16[128,576]{1,0:T(8,128)(2,1)} %get-tuple-element.112), kind=kOutput, calls=%fused_computation.55 | convolution fusion | flops 1077927936 | bytes 16957440 | tf_op jit(solution)/shard_map/cond/branch_1_fun/thj,kj->thk/dot_general | solution.py:34
  174.1 0.8 max.10
  174.8 0.9 fusion.36
  175.7 0.8 multiply_add_fusion.5
  176.5 10.6 %multiply_add_fusion.4 = f32[128,64,512]{2,0,1:T(8,128)} fusion(f32[128,64,512]{2,0,1:T(8,128)} %get-tuple-element.115, f32[128,64]{0,1:T(8,128)S(1)} %get-tuple-element.291, f32[128,64,128]{0,2,1:T(8,128)S(1)} %get-tuple-element.309, f32[128,64]{0,1:T(8,128)S(1)} %max.10, pred[128,128]{0,1:T(8,128)(4,1)S(1)} %get-tuple-element.110, ...), kind=kOutput, calls=%fused_computation.53 | convolution fusion | flops 1085276160 | bytes 37961728 | tf_op jit(solution)/shard_map/cond/branch_1_fun/thk,kj->thj/dot_general | solution.py:44
  187.1 0.6 copy.134
  187.7 19.1 %conditional.9 = ((f32[128,64]{0,1:T(8,128)S(1)}, f32[128,64,512]{2,0,1:T(8,128)})) conditional(s32[]{:T(128)} %convert_element_type.66, (f32[128,64]{0,1:T(8,128)S(1)}, f32[128,64,512]{2,0,1:T(8,128)}) %tuple.43, (pred[128,128]{0,1:T(8,128)(4,1)S(1)}, bf16[128,576]{1,0:T(8,128)(2,1)S(1)}, bf16[128,64,512]{0,2,1:T(8,128)(2,1)}, ...), branch_computations={%region_27.28_spmd, %region_28.31_spmd} | conditional | flops 2300592128 | bytes 65044504 | solution.py:75
  187.7 0.1 copy.82
  187.8 0.8 fusion.57
  188.6 5.2 %select_reduce_fusion.4 = (f32[128,64]{0,1:T(8,128)S(1)}, f32[128,64,128]{0,2,1:T(8,128)S(1)}) fusion(pred[128,128]{0,1:T(8,128)(4,1)S(1)} %get-tuple-element.118, f32[128,64,128]{0,2,1:T(8,128)S(1)} %fusion.57, bf16[128,64,512]{0,2,1:T(8,128)(2,1)} %get-tuple-element.274, bf16[128,576]{1,0:T(8,128)(2,1)S(1)} %get-tuple-element.120), kind=kOutput, calls=%fused_computation.73 | convolution fusion | flops 1077927936 | bytes 16957440 | tf_op jit(solution)/shard_map/cond/branch_1_fun/thj,kj->thk/dot_general | solution.py:34
  193.8 0.8 max.11
  194.5 0.9 fusion.48
  195.5 0.8 multiply_add_fusion.7
  196.2 10.6 %multiply_add_fusion.6 = f32[128,64,512]{2,0,1:T(8,128)} fusion(f32[128,64,512]{2,0,1:T(8,128)} %get-tuple-element.122, f32[128,64]{0,1:T(8,128)S(1)} %get-tuple-element.293, f32[128,64,128]{0,2,1:T(8,128)S(1)} %get-tuple-element.311, f32[128,64]{0,1:T(8,128)S(1)} %max.11, pred[128,128]{0,1:T(8,128)(4,1)S(1)} %get-tuple-element.118, ...), kind=kOutput, calls=%fused_computation.71 | convolution fusion | flops 1085276160 | bytes 37961728 | tf_op jit(solution)/shard_map/cond/branch_1_fun/thk,kj->thj/dot_general | solution.py:44
  206.8 11.9 %copy.95 = bf16[512,8192]{0,1:T(8,128)(2,1)} copy(bf16[512,8192]{1,0:T(8,128)(2,1)} %all-gather.5.cloned.1.call-done) | data formatting | bytes 16777216 | tf_op jit(solution)/shard_map/all_gather | solution.py:89
  218.7 11.1 %fusion.62 = bf16[64,128,128]{1,2,0:T(8,128)(2,1)} fusion(bf16[512,64,128]{0,2,1:T(8,128)(2,1)} %bitcast.85, f32[128,64,512]{2,0,1:T(8,128)} %get-tuple-element.149, f32[128,64]{0,1:T(8,128)S(1)} %get-tuple-element.150), kind=kOutput, calls=%fused_computation.94 | convolution fusion | flops 1083179008 | bytes 27295744 | tf_op jit(solution)/shard_map/thj,jhd->thd/dot_general | solution.py:92
  229.8 4.1 %copy.96 = bf16[128,8192]{1,0:T(8,128)(2,1)} copy(bf16[128,8192]{0,1:T(8,128)(2,1)} %bitcast.86) | data formatting | bytes 4194304 | tf_op jit(solution)/shard_map/convert_element_type | solution.py:94
  (24 shorter events, 0.1 us)
Async XLA Ops:
  6.5 93.9 %copy-start = (bf16[128,8192]{1,0:T(8,128)(2,1)S(1)}, bf16[128,8192]{1,0:T(8,128)(2,1)}, u32[]{:S(2)}) copy-start(bf16[128,8192]{1,0:T(8,128)(2,1)} %param.16) | copy-start | bytes 6291460
  6.5 82.0 %all-gather.3.cloned.1.call-start = ((), (), s32[]{:S(2)}) async-start(), calls=%async_computation | async-start | bytes 8912896 | tf_op jit(solution)/shard_map/all_gather | solution.py:59
  7.3 199.5 %all-gather.5.cloned.1.call-start = ((), (), s32[]{:S(2)}) async-start(), calls=%async_computation.1 | async-start | bytes 8912896 | tf_op jit(solution)/shard_map/all_gather | solution.py:89
  9.1 7.5 %collective-permute-start = (bf16[128,576]{1,0:T(8,128)(2,1)S(1)}, bf16[128,576]{1,0:T(8,128)(2,1)S(1)}, u32[]{:S(2)}, u32[]{:S(2)}) collective-permute-start(bf16[128,576]{1,0:T(8,128)(2,1)S(1)} %copy.90), channel_id=1, source_target_pairs={{0,1},{1,2},{2,3},{3,4},{4,5},{5,6},{6,7},{7,8},{8,9},{9,10},{10,1... | collective-permute-start | bytes 442376 | tf_op jit(solution)/shard_map/ppermute | solution.py:19
  16.6 10.6 %collective-permute-start.1 = (bf16[128,576]{1,0:T(8,128)(2,1)S(1)}, bf16[128,576]{1,0:T(8,128)(2,1)S(1)}, u32[]{:S(2)}, u32[]{:S(2)}) collective-permute-start(bf16[128,576]{1,0:T(8,128)(2,1)S(1)} %collective-permute-done), channel_id=1, source_target_pairs={{0,1},{1,2},{2,3},{3,4},{4,5},{5,6},{6,7},{7,8},{8,9},{9,10},{10,1... | collective-permute-start | bytes 442376 | tf_op jit(solution)/shard_map/ppermute | solution.py:19
  27.2 6.5 %copy-start.2 = (bf16[128,576]{1,0:T(8,128)(2,1)}, bf16[128,576]{1,0:T(8,128)(2,1)S(1)}, u32[]{:S(2)}) copy-start(bf16[128,576]{1,0:T(8,128)(2,1)S(1)} %collective-permute-done.1) | copy-start | bytes 442372
  27.2 11.1 %collective-permute-start.2 = (bf16[128,576]{1,0:T(8,128)(2,1)S(1)}, bf16[128,576]{1,0:T(8,128)(2,1)}, u32[]{:S(2)}, u32[]{:S(2)}) collective-permute-start(bf16[128,576]{1,0:T(8,128)(2,1)S(1)} %collective-permute-done.1), channel_id=1, source_target_pairs={{0,1},{1,2},{2,3},{3,4},{4,5},{5,6},{6,7},{7,8},{8,9},{9,10},{10,1... | collective-permute-start | bytes 442376 | tf_op jit(solution)/shard_map/ppermute | solution.py:19
  38.4 149.3 %collective-permute-start.3 = (bf16[128,576]{1,0:T(8,128)(2,1)}, bf16[128,576]{1,0:T(8,128)(2,1)S(1)}, u32[]{:S(2)}, u32[]{:S(2)}) collective-permute-start(bf16[128,576]{1,0:T(8,128)(2,1)} %collective-permute-done.2), channel_id=1, source_target_pairs={{0,1},{1,2},{2,3},{3,4},{4,5},{5,6},{6,7},{7,8},{8,9},{9,10},{10,1... | collective-permute-start | bytes 442376 | tf_op jit(solution)/shard_map/ppermute | solution.py:19
  107.3 19.2 %copy-start.4 = (pred[128,128]{0,1:T(8,128)(4,1)S(1)}, pred[128,128]{0,1:T(8,128)(4,1)}, u32[]{:S(2)}) copy-start(pred[128,128]{0,1:T(8,128)(4,1)} %get-tuple-element.317) | copy-start | bytes 49156
  107.3 2.6 %copy-start.5 = (pred[128,128]{0,1:T(8,128)(4,1)S(1)}, pred[128,128]{0,1:T(8,128)(4,1)}, u32[]{:S(2)}) copy-start(pred[128,128]{0,1:T(8,128)(4,1)} %get-tuple-element.91) | copy-start | bytes 49156 | tf_op jit(solution)/shard_map/cond
  126.5 20.2 %copy-start.3 = (bf16[128,576]{1,0:T(8,128)(2,1)S(1)}, bf16[128,576]{1,0:T(8,128)(2,1)}, u32[]{:S(2)}) copy-start(bf16[128,576]{1,0:T(8,128)(2,1)} %copy-done.2) | copy-start | bytes 442372
  218.7 15.2 %copy-start.1 = (bf16[128,8192]{1,0:T(8,128)(2,1)S(1)}, bf16[128,8192]{1,0:T(8,128)(2,1)}, u32[]{:S(2)}) copy-start(bf16[128,8192]{1,0:T(8,128)(2,1)} %param.16) | copy-start | bytes 6291460
Sparse Core Ops, SparseCore 0:
  9.5 78.9 all-gather.2
  90.7 73.3 all-gather.4
where the time goes:
time: 243 us; the launch traced here: 241 us
  matrix products  99.7 us (41%)
  waiting for transfers between devices  65.4 us (27%)
  local copies, waits for them, and re-layouts  35 us (14%)
  between operations  16.5 us (7%)
  other arithmetic  16.2 us (7%)
  starting transfers between devices  7.69 us (3%)
    dot_general x5, matrix products, attend(): jnp.einsum('thk,kj->thj', weights.astype(jnp.bfloat16), keys[:, :LAT], pr...  50.7 us
    all_gather x1, waiting for transfers between devices, shards(): piece = lax.all_gather(w_uk, 'ctx', axis=0, tiled=True)  48.3 us
    dot_general x5, matrix products, attend(): jnp.einsum('thj,kj->thk', absorbed, keys[:, :LAT], preferred_element_type...  26.7 us
    ppermute x4, waiting for transfers between devices, from_behind(): return lax.ppermute(block, axis, route)  15.7 us
    all_gather x1, local copies, waits for them, and re-layouts, shards(): piece = lax.all_gather(w_uv, 'ctx', axis=0, tiled=True)  11.9 us
    all_gather x1, local copies, waits for them, and re-layouts, shards(): piece = lax.all_gather(w_uk, 'ctx', axis=0, tiled=True)  11.9 us
    dot_general x1, matrix products, shards(): jnp.einsum('thj,jhd->thd', mixed, weights, preferred_element_type=jnp.flo...  11.1 us
    ppermute x4, starting transfers between devices, from_behind(): return lax.ppermute(block, axis, route)  7.65 us
  transfers between devices with their start and end apart: 6, of which 4 were waited for; matrix products, arithmetic and copies ran while one was open for 51% of the time, Pallas kernels for 0%

commit v1 on v0

--- a/solution.py
+++ b/solution.py
@@ -3,6 +3,8 @@
 import jax
 import jax.numpy as jnp
 from jax import lax
+from jax.experimental import pallas as pl
+from jax.experimental.pallas import tpu as pltpu
 from jax.sharding import PartitionSpec as P
 
 HEADS = 64
@@ -11,6 +13,9 @@
 DR = 64
 LAT = 512
 SPAN = 4
+MESH = pl.DeviceIdType.MESH
+Z_AHEAD = 4
+X_AHEAD = 2
 
 
 def from_behind(block, axis, distance):
@@ -94,6 +99,299 @@
     return result.astype(jnp.bfloat16)
 
 
+HG = 4
+SPREAD = 5
+
+
+def window_kernel(
+    qn_hbm, qr_hbm, lat_hbm, uk_hbm, uv_hbm, lens, out,
+    qn, qr, win, keys, bias, lhs, wts,
+    local_sem, lat_send, lat_recv, z_send, z_recv, x_send, x_recv, y_send, y_recv, c_send, c_recv,
+):
+    rows = qn_hbm.shape[0]
+    steps = HEADS // HG
+    cols = HG * DN
+    n = lax.axis_size("ctx")
+    group = lax.axis_index("groups")
+    place = lax.axis_index("ctx")
+    z = place // 4
+    x = (place // 2) % 2
+    c = place % 2
+    half = uk_hbm.shape[0] // 2
+    mine = pl.ds(pl.multiple_of(group * half, half), half)
+    theirs = pl.ds(pl.multiple_of((1 - group) * half, half), half)
+    weights = (uk_hbm, uv_hbm)
+
+    def at_ctx(i):
+        return (group, i)
+
+    x_peer = at_ctx((z * 2 + (1 - x)) * 2 + c)
+    c_peer = at_ctx((z * 2 + x) * 2 + (1 - c))
+    y_peer = (1 - group, place)
+
+    def plane(d):
+        return lax.rem(z + d, 4)
+
+    def z_peer(d):
+        return at_ctx((plane(d) * 2 + x) * 2 + c)
+
+    def chunk(k):
+        return pl.ds(pl.multiple_of(k * cols, cols), cols)
+
+    def remote(src, dst, send, recv, peer):
+        return pltpu.make_async_remote_copy(
+            src_ref=src, dst_ref=dst, send_sem=send, recv_sem=recv, device_id=peer, device_id_type=MESH
+        )
+
+    locals_ = [
+        pltpu.make_async_copy(lat_hbm, win.at[SPREAD - 1], local_sem.at[0]),
+        pltpu.make_async_copy(qn_hbm, qn, local_sem.at[1]),
+        pltpu.make_async_copy(qr_hbm, qr, local_sem.at[2]),
+    ]
+
+    def own(k, m):
+        return pltpu.make_async_copy(
+            weights[m].at[:, chunk(k)], wts.at[k, m, z, x, c], local_sem.at[3 + m * steps + k]
+        )
+
+    barrier = pltpu.get_barrier_semaphore()
+    offsets = (1, 2, 3, 4, 8, n - 4, n - 3, n - 2, n - 1)
+    for d in offsets:
+        pl.semaphore_signal(barrier, inc=1, device_id=at_ctx(lax.rem(place + d, n)), device_id_type=MESH)
+    pl.semaphore_signal(barrier, inc=1, device_id=y_peer, device_id_type=MESH)
+    for copy in locals_:
+        copy.start()
+
+    @pl.loop(0, steps)
+    def _(k):
+        own(k, 0).start()
+        own(k, 1).start()
+
+    pl.semaphore_wait(barrier, len(offsets) + 1)
+
+    def z_copy(k, d, m):
+        return remote(
+            weights[m].at[mine, chunk(k)], wts.at[k, m, z, x, c, mine], z_send.at[k, d - 1, m], z_recv.at[k, d - 1, m], z_peer(d)
+        )
+
+    def z_arrival(k, d, m):
+        slot = wts.at[k, m, plane(4 - d), x, c, mine]
+        return remote(slot, slot, z_send.at[k, d - 1, m], z_recv.at[k, d - 1, m], z_peer(d))
+
+    def x_own(k, m):
+        return remote(
+            weights[m].at[:, chunk(k)], wts.at[k, m, z, x, c], x_send.at[k, 3 + m], x_recv.at[k, 3 + m], x_peer
+        )
+
+    def x_own_arrival(k, m):
+        slot = wts.at[k, m, z, 1 - x, c]
+        return remote(slot, slot, x_send.at[k, 3 + m], x_recv.at[k, 3 + m], x_peer)
+
+    def x_copy(k, d):
+        slot = wts.at[k, :, plane(d), x, c, mine]
+        return remote(slot, slot, x_send.at[k, d - 1], x_recv.at[k, d - 1], x_peer)
+
+    def x_arrival(k, d):
+        slot = wts.at[k, :, plane(d), 1 - x, c, mine]
+        return remote(slot, slot, x_send.at[k, d - 1], x_recv.at[k, d - 1], x_peer)
+
+    def y_copy(k, d):
+        slot = wts.at[k, :, plane(d), :, c, mine]
+        return remote(slot, slot, y_send.at[k, d - 1], y_recv.at[k, d - 1], y_peer)
+
+    def y_arrival(k, d):
+        slot = wts.at[k, :, plane(d), :, c, theirs]
+        return remote(slot, slot, y_send.at[k, d - 1], y_recv.at[k, d - 1], y_peer)
+
+    def c_copy(k):
+        slot = wts.at[k, :, :, :, c]
+        return remote(slot, slot, c_send.at[k], c_recv.at[k], c_peer)
+
+    def c_arrival(k):
+        slot = wts.at[k, :, :, :, 1 - c]
+        return remote(slot, slot, c_send.at[k], c_recv.at[k], c_peer)
+
+    def lat_copy(d):
+        return remote(
+            lat_hbm, win.at[SPREAD - 1 - d], lat_send.at[d - 1], lat_recv.at[d - 1], at_ctx(lax.rem(place + d, n))
+        )
+
+    def start_z(k):
+        for d in (1, 3, 2):
+            for m in range(2):
+                z_copy(k, d, m).start()
+
+    def start_x_own(k):
+        for m in range(2):
+            x_own(k, m).start()
+
+    @pl.loop(0, X_AHEAD)
+    def _(k):
+        start_x_own(k)
+
+    @pl.loop(0, Z_AHEAD // 2)
+    def _(k):
+        start_z(k)
+
+    for d in range(1, SPREAD):
+        lat_copy(d).start()
+
+    @pl.loop(Z_AHEAD // 2, Z_AHEAD)
+    def _(k):
+        start_z(k)
+
+    q_pos = place * rows + lax.broadcasted_iota(jnp.int32, (rows, SPREAD * rows), 0)
+    k_pos = (place - (SPREAD - 1)) * rows + lax.broadcasted_iota(jnp.int32, (rows, SPREAD * rows), 1)
+    low = jnp.zeros_like(q_pos)
+    start = jnp.int32(0)
+    for e in range(lens.shape[0]):
+        low = jnp.where(q_pos >= start, start, low)
+        start = start + lens[e]
+    bias[...] = jnp.where((k_pos <= q_pos) & (k_pos >= low), jnp.float32(0.0), jnp.float32(-1e30))
+
+    for copy in locals_:
+        copy.wait()
+
+    @pl.loop(0, steps)
+    def _(k):
+        own(k, 0).wait()
+        own(k, 1).wait()
+
+    scale = math.log2(math.e) / math.sqrt(DN + DR)
+    nt = (((1,), (1,)), ((), ()))
+    lane = lax.broadcasted_iota(jnp.int32, (1, 2 * DR), 1)
+    sides = [
+        (lane < DR).astype(jnp.float32).astype(jnp.bfloat16),
+        (lane >= DR).astype(jnp.float32).astype(jnp.bfloat16),
+    ]
+
+    def attend_chunk(k):
+        for pair in range(HG // 2):
+            both = qr[:, pl.ds(pl.multiple_of((k * (HG // 2) + pair) * 2 * DR, 2 * DR), 2 * DR)]
+            for side in range(2):
+                i = pair * 2 + side
+                q = qn[:, pl.ds(pl.multiple_of(k * cols + i * DN, DN), DN)]
+                w = wts[k, 0, :, :, :, :, i * DN : (i + 1) * DN].reshape(LAT, DN)
+                a = lax.dot_general(q, w, nt, preferred_element_type=jnp.float32)
+                lhs[i * rows : (i + 1) * rows, :LAT] = a.astype(jnp.bfloat16)
+                lhs[i * rows : (i + 1) * rows, LAT:] = both * sides[side]
+        for pair in range(HG // 2):
+            part = lhs[pair * 2 * rows : (pair + 1) * 2 * rows, :]
+            s = lax.dot_general(part, keys[...], nt, preferred_element_type=jnp.float32)
+            s = s.reshape(2, rows, SPREAD * rows) * scale + bias[...][None]
+            s = s.reshape(2 * rows, SPREAD * rows)
+            p = jnp.exp2(s - jnp.max(s, axis=-1, keepdims=True))
+            total = jnp.sum(p, axis=-1, keepdims=True)
+            mixed = jnp.dot(p.astype(jnp.bfloat16), keys[:, :LAT], preferred_element_type=jnp.float32)
+            mixed = (mixed * (1.0 / total)).astype(jnp.bfloat16)
+            for side in range(2):
+                i = pair * 2 + side
+                w = wts[k, 1, :, :, :, :, i * DV : (i + 1) * DV].reshape(LAT, DV)
+                o = jnp.dot(mixed[side * rows : (side + 1) * rows], w, preferred_element_type=jnp.float32)
+                out[:, pl.ds(pl.multiple_of(k * cols + i * DV, DV), DV)] = o.astype(out.dtype)
+
+    @pl.loop(0, steps + 3)
+    def _(s):
+        @pl.when(s < steps)
+        def _():
+            for d in range(1, 4):
+                for m in range(2):
+                    z_arrival(s, d, m).wait_recv()
+            for d in range(1, 4):
+                x_copy(s, d).start()
+
+        @pl.when(s + X_AHEAD < steps)
+        def _():
+            start_x_own(s + X_AHEAD)
+
+        @pl.when(s + Z_AHEAD < steps)
+        def _():
+            start_z(s + Z_AHEAD)
+
+        @pl.when((s >= 1) & (s <= steps))
+        def _():
+            k = s - 1
+            for m in range(2):
+                x_own_arrival(k, m).wait_recv()
+            for d in range(1, 4):
+                x_arrival(k, d).wait_recv()
+            for d in range(1, 4):
+                y_copy(k, d).start()
+
+        @pl.when((s >= 2) & (s <= steps + 1))
+        def _():
+            k = s - 2
+            for d in range(1, 4):
+                y_arrival(k, d).wait_recv()
+            c_copy(k).start()
+
+        @pl.when(s == 2)
+        def _():
+            for d in range(1, SPREAD):
+                lat_copy(d).wait_recv()
+            for b in range(SPREAD):
+                block = win[b]
+                keys[b * rows : (b + 1) * rows, : LAT + DR] = block
+                keys[b * rows : (b + 1) * rows, LAT + DR :] = block[:, LAT:]
+
+        @pl.when(s >= 3)
+        def _():
+            k = s - 3
+            c_arrival(k).wait_recv()
+            attend_chunk(k)
+
+    for d in range(1, SPREAD):
+        lat_copy(d).wait_send()
+
+    @pl.loop(0, steps)
+    def _(k):
+        for d in range(1, 4):
+            for m in range(2):
+                z_copy(k, d, m).wait_send()
+            x_copy(k, d).wait_send()
+            y_copy(k, d).wait_send()
+        for m in range(2):
+            x_own(k, m).wait_send()
+        c_copy(k).wait_send()
+
+
+def kernel_shards(q_nope, q_rope, latent, w_uk, w_uv, doc_lengths):
+    rows = q_nope.shape[0]
+    steps = HEADS // HG
+    window = SPREAD * rows
+    anywhere = pl.BlockSpec(memory_space=pl.ANY)
+    dma = pltpu.SemaphoreType.DMA
+    return pl.pallas_call(
+        window_kernel,
+        out_shape=jax.ShapeDtypeStruct((rows, HEADS * DV), jnp.bfloat16),
+        in_specs=[anywhere] * 5 + [pl.BlockSpec(memory_space=pltpu.SMEM)],
+        out_specs=pl.BlockSpec(memory_space=pltpu.VMEM),
+        scratch_shapes=[
+            pltpu.VMEM(q_nope.shape, jnp.bfloat16),
+            pltpu.VMEM(q_rope.shape, jnp.bfloat16),
+            pltpu.VMEM((SPREAD, rows, LAT + DR), jnp.bfloat16),
+            pltpu.VMEM((window, LAT + 2 * DR), jnp.bfloat16),
+            pltpu.VMEM((rows, window), jnp.float32),
+            pltpu.VMEM((HG * rows, LAT + 2 * DR), jnp.bfloat16),
+            pltpu.VMEM((steps, 2, 4, 2, 2, w_uk.shape[0], HG * DN), jnp.bfloat16),
+            dma((3 + 2 * steps,)),
+            dma((SPREAD - 1,)),
+            dma((SPREAD - 1,)),
+            dma((steps, 3, 2)),
+            dma((steps, 3, 2)),
+            dma((steps, 5)),
+            dma((steps, 5)),
+            dma((steps, 3)),
+            dma((steps, 3)),
+            dma((steps,)),
+            dma((steps,)),
+        ],
+        compiler_params=pltpu.CompilerParams(
+            collective_id=0, has_side_effects=True, vmem_limit_bytes=48 * 1024 * 1024
+        ),
+    )(q_nope, q_rope, latent, w_uk, w_uv, doc_lengths)
+
+
 def solution(mesh):
     placed = (
         P(("groups", "ctx"), None),
@@ -103,6 +401,11 @@
         P("ctx", None),
         P("groups"),
     )
+    small = mesh.shape["ctx"] == 16 and mesh.shape["groups"] == 2
     return jax.shard_map(
-        shards, mesh=mesh, in_specs=placed, out_specs=P(("groups", "ctx"), None), check_vma=False
+        kernel_shards if small else shards,
+        mesh=mesh,
+        in_specs=placed,
+        out_specs=P(("groups", "ctx"), None),
+        check_vma=False,
     )

time: 243 us -> 114 us (0.47)
  the two profiles are of different devices: /device:TPU:8 before, /device:TPU:0 now
where the time goes in v1:
time: 114 us; the launch traced here: 113 us
  Pallas kernels  107 us (94%)
  local copies, waits for them, and re-layouts  6.34 us (6%)
    pallas_call x1, Pallas kernels, kernel_shards(): pl.pallas_call(window_kernel, out_shape=jax.ShapeDtypeStruct((rows, HEADS...  107 us
    unnamed x10, local copies, waits for them, and re-layouts  6.34 us

profile of v1, /device:TPU:0, one launch (start us, length us, event | category | flops | bytes accessed | tf_op | source)
XLA Modules:
  0.0 113.4 jit_solution(14093088253003575627)
XLA Ops:
  0.0 1.1 copy.7.lat_hbm
  1.1 0.0 copy-start
  1.1 1.2 %copy-done = bf16[128,4096]{1,0:T(8,128)(2,1)S(1)} copy-done((bf16[128,4096]{1,0:T(8,128)(2,1)S(1)}, bf16[128,4096]{1,0:T(8,128)(2,1)}, u32[]{:S(2)}) %copy-start) | copy-done | bytes 1048600
  2.3 0.0 copy-start.1
  2.3 1.0 copy-done.1
  3.3 0.0 copy-start.2
  3.3 1.0 copy-done.2
  4.4 0.0 copy-start.3
  4.4 0.7 copy-done.3
  5.0 107.1 %shard_map.64 = bf16[128,8192]{1,0:T(8,128)(2,1)S(1)} custom-call(bf16[128,8192]{1,0:T(8,128)(2,1)} %qn_hbm.1, bf16[128,4096]{1,0:T(8,128)(2,1)S(1)} %copy-done, bf16[128,576]{1,0:T(8,128)(2,1)S(1)} %copy.7.lat_hbm, bf16[32,8192]{1,0:T(8,128)(2,1)S(1)} %copy-done.1, bf16[32,8192]{1,0:T(8,128)(2,1)S(1)} %copy-done.2, s32[8]{0:T(128)S(1)} %copy-done.3), custom_call_target="tpu_custom_call" | custom-call | tf_op jit(solution)/shard_map/pallas_call | solution.py:364
  112.1 1.3 %copy.9 = bf16[128,8192]{1,0:T(8,128)(2,1)} copy(bf16[128,8192]{1,0:T(8,128)(2,1)S(1)} %shard_map.64) | data formatting | bytes 4194304
Async XLA Ops:
  1.1 1.2 %copy-start = (bf16[128,4096]{1,0:T(8,128)(2,1)S(1)}, bf16[128,4096]{1,0:T(8,128)(2,1)}, u32[]{:S(2)}) copy-start(bf16[128,4096]{1,0:T(8,128)(2,1)} %qr_hbm.1) | copy-start | bytes 3145732
  2.3 1.0 copy-start.1
  3.3 1.0 copy-start.2
  4.4 0.7 copy-start.3

commit v2 on v1

--- a/solution.py
+++ b/solution.py
@@ -14,8 +14,8 @@
 LAT = 512
 SPAN = 4
 MESH = pl.DeviceIdType.MESH
-Z_AHEAD = 4
-X_AHEAD = 2
+Z_AHEAD = 2
+X_AHEAD = 1
 
 
 def from_behind(block, axis, distance):
@@ -144,7 +144,7 @@
         )
 
     locals_ = [
-        pltpu.make_async_copy(lat_hbm, win.at[SPREAD - 1], local_sem.at[0]),
+        pltpu.make_async_copy(lat_hbm, win.at[2, c], local_sem.at[0]),
         pltpu.make_async_copy(qn_hbm, qn, local_sem.at[1]),
         pltpu.make_async_copy(qr_hbm, qr, local_sem.at[2]),
     ]
@@ -155,7 +155,7 @@
         )
 
     barrier = pltpu.get_barrier_semaphore()
-    offsets = (1, 2, 3, 4, 8, n - 4, n - 3, n - 2, n - 1)
+    offsets = (1, 2, 4, 8, n - 4, n - 2, n - 1)
     for d in offsets:
         pl.semaphore_signal(barrier, inc=1, device_id=at_ctx(lax.rem(place + d, n)), device_id_type=MESH)
     pl.semaphore_signal(barrier, inc=1, device_id=y_peer, device_id_type=MESH)
@@ -195,13 +195,29 @@
         slot = wts.at[k, :, plane(d), 1 - x, c, mine]
         return remote(slot, slot, x_send.at[k, d - 1], x_recv.at[k, d - 1], x_peer)
 
+    def x_relay(k):
+        slot = wts.at[k, 1, plane(3), x, c, theirs]
+        return remote(slot, slot, x_send.at[k, 5], x_recv.at[k, 5], x_peer)
+
+    def x_relay_arrival(k):
+        slot = wts.at[k, 1, plane(3), 1 - x, c, theirs]
+        return remote(slot, slot, x_send.at[k, 5], x_recv.at[k, 5], x_peer)
+
     def y_copy(k, d):
-        slot = wts.at[k, :, plane(d), :, c, mine]
+        slot = wts.at[k, :, plane(d), x, c, mine]
         return remote(slot, slot, y_send.at[k, d - 1], y_recv.at[k, d - 1], y_peer)
 
     def y_arrival(k, d):
-        slot = wts.at[k, :, plane(d), :, c, theirs]
+        slot = wts.at[k, :, plane(d), x, c, theirs]
         return remote(slot, slot, y_send.at[k, d - 1], y_recv.at[k, d - 1], y_peer)
+
+    def y_relay(k, d):
+        slot = wts.at[k, :, plane(d), 1 - x, c, mine] if d < 3 else wts.at[k, 0, plane(d), 1 - x, c, mine]
+        return remote(slot, slot, y_send.at[k, d + 2], y_recv.at[k, d + 2], y_peer)
+
+    def y_relay_arrival(k, d):
+        slot = wts.at[k, :, plane(d), 1 - x, c, theirs] if d < 3 else wts.at[k, 0, plane(d), 1 - x, c, theirs]
+        return remote(slot, slot, y_send.at[k, d + 2], y_recv.at[k, d + 2], y_peer)
 
     def c_copy(k):
         slot = wts.at[k, :, :, :, c]
@@ -212,9 +228,16 @@
         return remote(slot, slot, c_send.at[k], c_recv.at[k], c_peer)
 
     def lat_copy(d):
-        return remote(
-            lat_hbm, win.at[SPREAD - 1 - d], lat_send.at[d - 1], lat_recv.at[d - 1], at_ctx(lax.rem(place + d, n))
-        )
+        slot = win.at[2 - d, c]
+        return remote(lat_hbm, slot, lat_send.at[d], lat_recv.at[d], at_ctx(lax.rem(place + 2 * d, n)))
+
+    def lat_swap():
+        slot = win.at[:, c]
+        return remote(slot, slot, lat_send.at[0], lat_recv.at[0], c_peer)
+
+    def lat_swap_arrival():
+        slot = win.at[:, 1 - c]
+        return remote(slot, slot, lat_send.at[0], lat_recv.at[0], c_peer)
 
     def start_z(k):
         for d in (1, 3, 2):
@@ -225,20 +248,16 @@
         for m in range(2):
             x_own(k, m).start()
 
+    @pl.loop(0, Z_AHEAD)
+    def _(k):
+        start_z(k)
+
     @pl.loop(0, X_AHEAD)
     def _(k):
         start_x_own(k)
 
-    @pl.loop(0, Z_AHEAD // 2)
-    def _(k):
-        start_z(k)
-
-    for d in range(1, SPREAD):
+    for d in range(1, 3):
         lat_copy(d).start()
-
-    @pl.loop(Z_AHEAD // 2, Z_AHEAD)
-    def _(k):
-        start_z(k)
 
     q_pos = place * rows + lax.broadcasted_iota(jnp.int32, (rows, SPREAD * rows), 0)
     k_pos = (place - (SPREAD - 1)) * rows + lax.broadcasted_iota(jnp.int32, (rows, SPREAD * rows), 1)
@@ -277,12 +296,12 @@
                 lhs[i * rows : (i + 1) * rows, LAT:] = both * sides[side]
         for pair in range(HG // 2):
             part = lhs[pair * 2 * rows : (pair + 1) * 2 * rows, :]
-            s = lax.dot_general(part, keys[...], nt, preferred_element_type=jnp.float32)
+            s = jnp.dot(part, keys[...], preferred_element_type=jnp.float32)
             s = s.reshape(2, rows, SPREAD * rows) * scale + bias[...][None]
             s = s.reshape(2 * rows, SPREAD * rows)
             p = jnp.exp2(s - jnp.max(s, axis=-1, keepdims=True))
             total = jnp.sum(p, axis=-1, keepdims=True)
-            mixed = jnp.dot(p.astype(jnp.bfloat16), keys[:, :LAT], preferred_element_type=jnp.float32)
+            mixed = lax.dot_general(p.astype(jnp.bfloat16), keys[:LAT, :], nt, preferred_element_type=jnp.float32)
             mixed = (mixed * (1.0 / total)).astype(jnp.bfloat16)
             for side in range(2):
                 i = pair * 2 + side
@@ -290,76 +309,93 @@
                 o = jnp.dot(mixed[side * rows : (side + 1) * rows], w, preferred_element_type=jnp.float32)
                 out[:, pl.ds(pl.multiple_of(k * cols + i * DV, DV), DV)] = o.astype(out.dtype)
 
-    @pl.loop(0, steps + 3)
-    def _(s):
-        @pl.when(s < steps)
-        def _():
-            for d in range(1, 4):
-                for m in range(2):
-                    z_arrival(s, d, m).wait_recv()
-            for d in range(1, 4):
-                x_copy(s, d).start()
-
-        @pl.when(s + X_AHEAD < steps)
-        def _():
-            start_x_own(s + X_AHEAD)
-
-        @pl.when(s + Z_AHEAD < steps)
-        def _():
-            start_z(s + Z_AHEAD)
-
-        @pl.when((s >= 1) & (s <= steps))
-        def _():
-            k = s - 1
-            for m in range(2):
-                x_own_arrival(k, m).wait_recv()
-            for d in range(1, 4):
-                x_arrival(k, d).wait_recv()
-            for d in range(1, 4):
-                y_copy(k, d).start()
-
-        @pl.when((s >= 2) & (s <= steps + 1))
-        def _():
-            k = s - 2
-            for d in range(1, 4):
-                y_arrival(k, d).wait_recv()
-            c_copy(k).start()
-
-        @pl.when(s == 2)
-        def _():
-            for d in range(1, SPREAD):
-                lat_copy(d).wait_recv()
-            for b in range(SPREAD):
-                block = win[b]
-                keys[b * rows : (b + 1) * rows, : LAT + DR] = block
-                keys[b * rows : (b + 1) * rows, LAT + DR :] = block[:, LAT:]
-
-        @pl.when(s >= 3)
-        def _():
-            k = s - 3
-            c_arrival(k).wait_recv()
-            attend_chunk(k)
-
-    for d in range(1, SPREAD):
-        lat_copy(d).wait_send()
-
-    @pl.loop(0, steps)
-    def _(k):
+    def finish(k):
         for d in range(1, 4):
             for m in range(2):
                 z_copy(k, d, m).wait_send()
             x_copy(k, d).wait_send()
             y_copy(k, d).wait_send()
+            y_relay(k, d).wait_send()
         for m in range(2):
             x_own(k, m).wait_send()
+        x_relay(k).wait_send()
         c_copy(k).wait_send()
+
+    @pl.loop(0, steps + 3)
+    def _(s):
+        @pl.when(s < steps)
+        def _():
+            for d in (1, 3, 2):
+                for m in range(2):
+                    z_arrival(s, 4 - d, m).wait_recv()
+                x_copy(s, d).start()
+                y_copy(s, d).start()
+
+        @pl.when(s + X_AHEAD < steps)
+        def _():
+            start_x_own(s + X_AHEAD)
+
+        @pl.when(s + Z_AHEAD < steps)
+        def _():
+            start_z(s + Z_AHEAD)
+
+        @pl.when((s >= 1) & (s <= steps))
+        def _():
+            k = s - 1
+            for d in range(1, 4):
+                x_arrival(k, d).wait_recv()
+                y_relay(k, d).start()
+            for d in range(1, 4):
+                y_arrival(k, d).wait_recv()
+            x_relay(k).start()
+
+        @pl.when((s >= 2) & (s <= steps + 1))
+        def _():
+            k = s - 2
+            for m in range(2):
+                x_own_arrival(k, m).wait_recv()
+            x_relay_arrival(k).wait_recv()
+            for d in range(1, 4):
+                y_relay_arrival(k, d).wait_recv()
+            c_copy(k).start()
+
+        @pl.when(s == 2)
+        def _():
+            for d in range(1, 3):
+                lat_copy(d).wait_recv()
+            lat_swap().start()
+
+        @pl.when(s == 3)
+        def _():
+            lat_swap_arrival().wait_recv()
+            for b in range(SPREAD):
+                span = slice(b * rows, (b + 1) * rows)
+                block = win[(b + c) // 2, (b + c) % 2]
+                keys[: LAT + DR, span] = block
+                keys[LAT + DR :, span] = block[LAT:]
+
+        @pl.when(s >= 4)
+        def _():
+            finish(s - 4)
+
+        @pl.when(s >= 3)
+        def _():
+            k = s - 3
+            c_arrival(k).wait_recv()
+            attend_chunk(k)
+
+    for d in range(1, 3):
+        lat_copy(d).wait_send()
+    lat_swap().wait_send()
+
+    finish(steps - 1)
 
 
 def kernel_shards(q_nope, q_rope, latent, w_uk, w_uv, doc_lengths):
     rows = q_nope.shape[0]
     steps = HEADS // HG
     window = SPREAD * rows
-    anywhere = pl.BlockSpec(memory_space=pl.ANY)
+    anywhere = pl.BlockSpec(memory_space=pltpu.HBM)
     dma = pltpu.SemaphoreType.DMA
     return pl.pallas_call(
         window_kernel,
@@ -369,27 +405,27 @@
         scratch_shapes=[
             pltpu.VMEM(q_nope.shape, jnp.bfloat16),
             pltpu.VMEM(q_rope.shape, jnp.bfloat16),
-            pltpu.VMEM((SPREAD, rows, LAT + DR), jnp.bfloat16),
-            pltpu.VMEM((window, LAT + 2 * DR), jnp.bfloat16),
+            pltpu.VMEM((3, 2, LAT + DR, rows), jnp.bfloat16),
+            pltpu.VMEM((LAT + 2 * DR, window), jnp.bfloat16),
             pltpu.VMEM((rows, window), jnp.float32),
             pltpu.VMEM((HG * rows, LAT + 2 * DR), jnp.bfloat16),
             pltpu.VMEM((steps, 2, 4, 2, 2, w_uk.shape[0], HG * DN), jnp.bfloat16),
             dma((3 + 2 * steps,)),
-            dma((SPREAD - 1,)),
-            dma((SPREAD - 1,)),
+            dma((3,)),
+            dma((3,)),
             dma((steps, 3, 2)),
             dma((steps, 3, 2)),
-            dma((steps, 5)),
-            dma((steps, 5)),
-            dma((steps, 3)),
-            dma((steps, 3)),
+            dma((steps, 6)),
+            dma((steps, 6)),
+            dma((steps, 6)),
+            dma((steps, 6)),
             dma((steps,)),
             dma((steps,)),
         ],
         compiler_params=pltpu.CompilerParams(
-            collective_id=0, has_side_effects=True, vmem_limit_bytes=48 * 1024 * 1024
+            collective_id=0, has_side_effects=True, vmem_limit_bytes=56 * 1024 * 1024
         ),
-    )(q_nope, q_rope, latent, w_uk, w_uv, doc_lengths)
+    )(q_nope, q_rope, latent.T, w_uk, w_uv, doc_lengths)
 
 
 def solution(mesh):

time: 114 us -> 99.4 us (0.87)
  Pallas kernels: 107 us -> 96.1 us
  local copies, waits for them, and re-layouts: 6.34 us -> 3.1 us
    pallas_call x1, Pallas kernels: 107 us -> 96.1 us  [kernel_shards(): pl.pallas_call(window_kernel, out_shape=jax.ShapeDtypeStruct((rows, HEADS...]
    unnamed x10 -> x1, local copies, waits for them, and re-layouts: 6.34 us -> 3.1 us
where the time goes in v2:
time: 99.4 us; the launch traced here: 99.3 us
  Pallas kernels  96.1 us (97%)
  local copies, waits for them, and re-layouts  3.1 us (3%)
    pallas_call x1, Pallas kernels, kernel_shards(): pl.pallas_call(window_kernel, out_shape=jax.ShapeDtypeStruct((rows, HEADS...  96.1 us
    unnamed x1, local copies, waits for them, and re-layouts  3.1 us

profile of v2, /device:TPU:0, one launch (start us, length us, event | category | flops | bytes accessed | tf_op | source)
XLA Modules:
  0.0 99.3 jit_solution(16681822874860045486)
XLA Ops:
  0.0 96.1 %shard_map.64 = bf16[128,8192]{1,0:T(8,128)(2,1)} custom-call(bf16[128,8192]{1,0:T(8,128)(2,1)} %qn_hbm.1, bf16[128,4096]{1,0:T(8,128)(2,1)} %qr_hbm.1, bf16[576,128]{1,0:T(8,128)(2,1)} %bitcast.1, bf16[32,8192]{1,0:T(8,128)(2,1)} %uk_hbm.1, bf16[32,8192]{1,0:T(8,128)(2,1)} %uv_hbm.1, s32[8]{0:T(128)} %lens.1), custom_call_target="tpu_custom_call" | custom-call | tf_op jit(solution)/shard_map/pallas_call | solution.py:400
  96.2 3.1 %copy.8 = bf16[128,8192]{1,0:T(8,128)(2,1)} copy(bf16[128,8192]{1,0:T(8,128)(2,1)} %shard_map.64) | data formatting | bytes 4194304

commit v3 on v2

--- a/solution.py
+++ b/solution.py
@@ -240,7 +240,7 @@
         return remote(slot, slot, lat_send.at[0], lat_recv.at[0], c_peer)
 
     def start_z(k):
-        for d in (1, 3, 2):
+        for d in (2, 1, 3):
             for m in range(2):
                 z_copy(k, d, m).start()
 
@@ -248,6 +248,9 @@
         for m in range(2):
             x_own(k, m).start()
 
+    for d in range(1, 3):
+        lat_copy(d).start()
+
     @pl.loop(0, Z_AHEAD)
     def _(k):
         start_z(k)
@@ -255,9 +258,6 @@
     @pl.loop(0, X_AHEAD)
     def _(k):
         start_x_own(k)
-
-    for d in range(1, 3):
-        lat_copy(d).start()
 
     q_pos = place * rows + lax.broadcasted_iota(jnp.int32, (rows, SPREAD * rows), 0)
     k_pos = (place - (SPREAD - 1)) * rows + lax.broadcasted_iota(jnp.int32, (rows, SPREAD * rows), 1)

time: 99.4 us -> 97.7 us (0.983)
  Pallas kernels: 96.1 us -> 94.2 us
    pallas_call x1, Pallas kernels: 96.1 us -> 94.2 us  [kernel_shards(): pl.pallas_call(window_kernel, out_shape=jax.ShapeDtypeStruct((rows, HEADS...]
where the time goes in v3:
time: 97.7 us; the launch traced here: 97.3 us
  Pallas kernels  94.2 us (96%)
  local copies, waits for them, and re-layouts  3.1 us (3%)
    pallas_call x1, Pallas kernels, kernel_shards(): pl.pallas_call(window_kernel, out_shape=jax.ShapeDtypeStruct((rows, HEADS...  94.2 us
    unnamed x1, local copies, waits for them, and re-layouts  3.1 us

profile of v3, /device:TPU:0, one launch (start us, length us, event | category | flops | bytes accessed | tf_op | source)
XLA Modules:
  0.0 97.3 jit_solution(10545866138550006865)
XLA Ops:
  0.0 94.2 %shard_map.64 = bf16[128,8192]{1,0:T(8,128)(2,1)} custom-call(bf16[128,8192]{1,0:T(8,128)(2,1)} %qn_hbm.1, bf16[128,4096]{1,0:T(8,128)(2,1)} %qr_hbm.1, bf16[576,128]{1,0:T(8,128)(2,1)} %bitcast.1, bf16[32,8192]{1,0:T(8,128)(2,1)} %uk_hbm.1, bf16[32,8192]{1,0:T(8,128)(2,1)} %uv_hbm.1, s32[8]{0:T(128)} %lens.1), custom_call_target="tpu_custom_call" | custom-call | tf_op jit(solution)/shard_map/pallas_call | solution.py:400
  94.2 3.1 %copy.8 = bf16[128,8192]{1,0:T(8,128)(2,1)} copy(bf16[128,8192]{1,0:T(8,128)(2,1)} %shard_map.64) | data formatting | bytes 4194304
